TPU v7x, 768 devices: a whole 4x8x12 slice. The times are simulated.
768 devices in a mesh: fsdp: 96 (over y_lo, z, x), group: 8 (over y_hi, core).
Axes of the slice: x: 4, y: 8 (y_hi: 4, y_lo: 2; y = y_hi * 2 + y_lo), z: 12, core: 2. Of those that a mesh axis runs over, the one named last changes fastest.
Arguments:
- query_rows: bfloat16 [96, 8, 128, 3072], P('fsdp', 'group'), may hold values from -40 to 40
- key_rows: bfloat16 [96, 8, 128, 3072], P('fsdp', 'group'), may hold values from -40 to 40
- value_rows: bfloat16 [96, 8, 128, 3072], P('fsdp', 'group'), may hold values from -6 to 6
- out_grad: bfloat16 [96, 8, 152, 3072], P('fsdp', 'group'), may hold values from -12 to 12
- query_gain: float32 [3072], P('fsdp'), may hold values from 0.5 to 1.5
- key_gain: float32 [3072], P('fsdp'), may hold values from 0.5 to 1.5
- image_sizes: int32 [96, 8, 4], P('fsdp', 'group'), may hold values from 16 to 72, as said below
- sends_tail: int32 [96, 8], P('fsdp', 'group'), may hold values from 0 to 1, as said below
Outputs:
- d_query: bfloat16 [96, 8, 128, 3072], P('fsdp', 'group')
- d_key: bfloat16 [96, 8, 128, 3072], P('fsdp', 'group')
- d_query_gain: float32 [3072], P('fsdp')
- d_key_gain: float32 [3072], P('fsdp')
Inputs may be any that keep to these rules, and one draw needn't show every extreme that they name: `image_sizes`: the last image of every shard has exactly 24 patches, the others 16 or more; each shard's images together fill its 128 rows. `sends_tail`: of a shard and its partner exactly one holds 1: the one whose images' squared patch counts sum larger, on equal sums the one of lower group index.
All inputs are finite; a program needn't handle non-finite values.
Results may differ from a plain program's by a relative error of at most 0.0069.
Values may be sent and summed in bfloat16 or wider, within the bound.
A program may use at most 32 MiB of HBM per device.

v0:
```python
import jax
import jax.numpy as jnp
from jax import lax
from jax.sharding import PartitionSpec as P

DH = 128


EPSILON = 1e-06


def swapped(value, axis, distance):
    return lax.ppermute(value, axis, [(i, i ^ 1 << distance) for i in range(lax.axis_size(axis))])


def normalize(values):
    center = values - jnp.mean(values, axis=-1, keepdims=True)
    inverse = lax.rsqrt(jnp.mean(center * center, axis=-1, keepdims=True) + EPSILON)
    return (center * inverse, inverse)


def norm_backward(grad_hat, row_hat, inverse):
    mean_grad = jnp.mean(grad_hat, axis=-1, keepdims=True)
    mean_cross = jnp.mean(grad_hat * row_hat, axis=-1, keepdims=True)
    return (grad_hat - mean_grad - row_hat * mean_cross) * inverse


def attend(buf_query, buf_key, buf_value, buf_grad, gain_query, gain_key, row_ids):
    row_count = buf_query.shape[0]
    head_count = buf_query.shape[1] // DH
    score_scale = DH ** (-0.5)
    query_hat, query_inv = normalize(
        buf_query.reshape(row_count, head_count, DH).astype(jnp.float32)
    )
    key_hat, key_inv = normalize(buf_key.reshape(row_count, head_count, DH).astype(jnp.float32))
    gain_q = gain_query.reshape(head_count, DH)
    gain_k = gain_key.reshape(head_count, DH)
    query_norm = (query_hat * gain_q).astype(jnp.bfloat16)
    key_norm = (key_hat * gain_k).astype(jnp.bfloat16)
    scores = (
        jnp.einsum("qhd,khd->hqk", query_norm, key_norm, preferred_element_type=jnp.float32)
        * score_scale
    )
    same_image = ((row_ids[:, None] == row_ids[None, :]) & (row_ids[:, None] >= 0)).astype(
        jnp.float32
    )
    live_rows = (row_ids >= 0).astype(jnp.float32)
    weights = jnp.exp(scores) * same_image[None, :, :]
    attention = weights / (jnp.sum(weights, axis=-1) + (1.0 - live_rows)[None, :])[:, :, None]
    value_heads = buf_value.reshape(row_count, head_count, DH)
    grad_heads = buf_grad.reshape(row_count, head_count, DH)
    grad_probs = jnp.einsum(
        "qhd,khd->hqk", grad_heads, value_heads, preferred_element_type=jnp.float32
    )
    carried = jnp.sum(attention * grad_probs, axis=-1)
    grad_scores = (attention * (grad_probs - carried[:, :, None]) * score_scale).astype(
        jnp.bfloat16
    )
    grad_qn = jnp.einsum("hqk,khd->qhd", grad_scores, key_norm, preferred_element_type=jnp.float32)
    grad_kn = jnp.einsum(
        "hqk,qhd->khd", grad_scores, query_norm, preferred_element_type=jnp.float32
    )
    grad_query = norm_backward(grad_qn * gain_q, query_hat, query_inv)
    grad_key = norm_backward(grad_kn * gain_k, key_hat, key_inv)
    term_query = jnp.sum(grad_qn * query_hat, axis=0).reshape(-1)
    term_key = jnp.sum(grad_kn * key_hat, axis=0).reshape(-1)
    return (
        grad_query.reshape(row_count, -1).astype(jnp.bfloat16),
        grad_key.reshape(row_count, -1).astype(jnp.bfloat16),
        term_query,
        term_key,
    )


def image_ids(size_list, row_count):
    image_ends = jnp.cumsum(size_list)
    places = jnp.arange(row_count, dtype=jnp.int32)
    return jnp.sum((places[:, None] >= image_ends[None, :]).astype(jnp.int32), axis=1)


def body(query_rows, key_rows, value_rows, out_grad, query_gain, key_gain, image_sizes, sends_tail):
    row_count = query_rows.shape[2]
    send_rows = out_grad.shape[2] - row_count
    head_rows = row_count - send_rows
    last_image = image_sizes.shape[-1] - 1
    pair_bit = lax.axis_size("group").bit_length() - 2
    full_gain_query, full_gain_key = (
        lax.all_gather(query_gain, "fsdp", axis=0, tiled=True),
        lax.all_gather(key_gain, "fsdp", axis=0, tiled=True),
    )
    is_sender = sends_tail[0, 0]
    own_query = query_rows[0, 0]
    own_key = key_rows[0, 0]
    own_value = value_rows[0, 0]
    grad_rows = out_grad[0, 0]
    own_ids = image_ids(image_sizes[0, 0], row_count)
    moved_rows = swapped(
        (own_query[head_rows:], own_key[head_rows:], own_value[head_rows:]), "group", pair_bit
    )
    kept_ids = jnp.where((is_sender == 1) & (own_ids == last_image), -1, own_ids)
    extra_ids = jnp.full((send_rows,), last_image + 1, jnp.int32) * (1 - is_sender) - is_sender
    row_ids = jnp.concatenate([kept_ids, extra_ids])
    grad_query, grad_key, term_query, term_key = attend(
        jnp.concatenate([own_query, moved_rows[0]]),
        jnp.concatenate([own_key, moved_rows[1]]),
        jnp.concatenate([own_value, moved_rows[2]]),
        grad_rows,
        full_gain_query,
        full_gain_key,
        row_ids,
    )
    returned = swapped((grad_query[row_count:], grad_key[row_count:]), "group", pair_bit)
    tail_query = jnp.where(is_sender == 1, returned[0], grad_query[head_rows:row_count])
    tail_key = jnp.where(is_sender == 1, returned[1], grad_key[head_rows:row_count])
    d_query = jnp.concatenate([grad_query[:head_rows], tail_query])
    d_key = jnp.concatenate([grad_key[:head_rows], tail_key])
    summed = lax.psum((term_query, term_key), "group")
    gain_grads = (
        lax.psum_scatter(summed[0], "fsdp", scatter_dimension=0, tiled=True),
        lax.psum_scatter(summed[1], "fsdp", scatter_dimension=0, tiled=True),
    )
    return (d_query[None, None], d_key[None, None], gain_grads[0], gain_grads[1])


def solution(mesh):
    placed = (
        P("fsdp", "group", None, None),
        P("fsdp", "group", None, None),
        P("fsdp", "group", None, None),
        P("fsdp", "group", None, None),
        P("fsdp"),
        P("fsdp"),
        P("fsdp", "group", None),
        P("fsdp", "group"),
    )
    return jax.shard_map(
        body,
        mesh=mesh,
        in_specs=placed,
        out_specs=(
            P("fsdp", "group", None, None),
            P("fsdp", "group", None, None),
            P("fsdp"),
            P("fsdp"),
        ),
        check_vma=False,
    )
```

profile of v0, /device:TPU:1, one launch (start us, length us, event | category | flops | bytes accessed | tf_op | source)
XLA Modules:
  0.0 1029.0 jit_solution(4538744181550242790)
XLA Ops:
  0.6 1.7 slice_bitcast_fusion.7
  2.3 8.4 collective-permute-start.1
  10.7 1.6 slice_bitcast_fusion.6
  12.3 1.9 collective-permute-start.2
  14.2 1.6 slice_bitcast_fusion.8
  15.8 7.3 collective-permute-start
  23.1 1.5 copy.51
  25.9 1.5 copy.48
  27.8 1.2 copy.55
  29.0 1.4 copy.75
  30.8 1.4 fusion.56
  33.4 385.6 %all-reduce.6 = (f32[3072]{0:T(1024)S(1)}, f32[3072]{0:T(1024)S(1)}) all-reduce(f32[3072]{0:T(1024)S(1)} %dynamic-update-slice, f32[3072]{0:T(1024)S(1)} %dynamic-update-slice.1), channel_id=1, replica_groups=mesh['fsdp'=96,'group'=8] {'fsdp'}, use_global_device_ids=true, to_apply=%add.1 | all-reduce | flops 6144 | bytes 49152
  421.2 1.6 fusion.24
  424.3 1.6 fusion.31
  426.0 4.6 fusion.5
  430.6 2.5 fusion.37
  433.2 12.0 %fusion.23 = (f32[24,128]{1,0:T(8,128)S(1)}, f32[152,24]{0,1:T(8,128)S(1)}, f32[152,24]{0,1:T(8,128)S(1)}, f32[24,128,152]{1,2,0:T(8,128)}) fusion(f32[152,24]{0,1:T(8,128)S(1)} %add_rsqrt_fusion, f32[152,24]{0,1:T(8,128)S(1)} %broadcast_multiply_fusion.4, bf16[24,24,128]{2,0,1:T(8,128)(2,1)S(1)} %copy_bitcast_fusion.5, ...), kind=kOutput, calls=%fused_computation.30 | convolution fusion | flops 157382736 | bytes 8402944 | tf_op jit(solution)/shard_map/hqk,khd->qhd/dot_general | solution.py:59
  445.2 4.6 fusion.22
  449.9 10.5 %fusion.30 = (f32[24,128]{1,0:T(8,128)S(1)}, f32[152,24]{0,1:T(8,128)S(1)}, f32[152,24]{0,1:T(8,128)S(1)}, f32[24,128,152]{1,2,0:T(8,128)}) fusion(f32[152,24]{0,1:T(8,128)S(1)} %add_rsqrt_fusion.1, f32[152,24]{0,1:T(8,128)S(1)} %broadcast_multiply_fusion.5, bf16[24,24,128]{2,0,1:T(8,128)(2,1)S(1)} %copy_bitcast_fusion.6, ...), kind=kOutput, calls=%fused_computation.37 | convolution fusion | flops 157382736 | bytes 8402944 | tf_op jit(solution)/shard_map/hqk,qhd->khd/dot_general | solution.py:60
  460.4 2.6 collective-permute-start.3
  463.1 4.6 fusion.29
  467.8 6.6 collective-permute-start.4
  474.4 371.3 %all-reduce.5 = (f32[3072]{0:T(1024)S(1)}, f32[3072]{0:T(1024)S(1)}) all-reduce(f32[3072]{0:T(1024)S(1)} %bitcast.133, f32[3072]{0:T(1024)S(1)} %bitcast.134), channel_id=2, replica_groups=mesh['fsdp'=96,'group'=8] {'fsdp'}, use_global_device_ids=true, to_apply=%region_14.15.clone | all-reduce | flops 6144 | bytes 49152
  845.9 181.2 %all-reduce.7 = (f32[32]{0:T(128)}, f32[32]{0:T(128)}) all-reduce(f32[32]{0:T(128)S(1)} %dynamic-slice.3, f32[32]{0:T(128)S(1)} %dynamic-slice.5), channel_id=1, replica_groups=mesh['fsdp'=96,'group'=8] {'group'}, use_global_device_ids=true, to_apply=%region_13.14 | all-reduce | flops 64 | bytes 512 | tf_op jit(solution)/shard_map/psum | solution.py:117
  (52 shorter events, 7.3 us)
Async XLA Ops:
  0.6 24.0 %copy-start.1 = (bf16[1,1,128,3072]{3,2,1,0:T(8,128)(2,1)S(1)}, bf16[1,1,128,3072]{3,2,1,0:T(8,128)(2,1)}, u32[]{:S(2)}) copy-start(bf16[1,1,128,3072]{3,2,1,0:T(8,128)(2,1)} %param.10) | copy-start | bytes 2359300
  2.3 22.7 %copy-start.2 = (s32[1,1,4]{2,1,0:T(1,128)S(1)}, s32[1,1,4]{2,1,0:T(1,128)}, u32[]{:S(2)}) copy-start(s32[1,1,4]{2,1,0:T(1,128)} %param.14) | copy-start | bytes 52
  2.3 417.4 %collective-permute-start.1 = (bf16[24,3072]{1,0:T(8,128)(2,1)}, bf16[24,3072]{1,0:T(8,128)(2,1)}, u32[]{:S(2)}, u32[]{:S(2)}) collective-permute-start(bf16[24,3072]{1,0:T(8,128)(2,1)} %slice_bitcast_fusion.7), channel_id=1, source_target_pairs={{0,4},{1,5},{2,6},{3,7},{4,0},{5,1},{6,2},{7,3},{8,12},{9,13},{10,... | collective-permute-start | bytes 442376 | tf_op jit(solution)/shard_map/ppermute | solution.py:13
  12.3 418.3 %collective-permute-start.2 = (bf16[24,3072]{1,0:T(8,128)(2,1)}, bf16[24,3072]{1,0:T(8,128)(2,1)S(1)}, u32[]{:S(2)}, u32[]{:S(2)}) collective-permute-start(bf16[24,3072]{1,0:T(8,128)(2,1)} %slice_bitcast_fusion.6), channel_id=1, source_target_pairs={{0,4},{1,5},{2,6},{3,7},{4,0},{5,1},{6,2},{7,3},{8,12},{9,13},{10,... | collective-permute-start | bytes 442376 | tf_op jit(solution)/shard_map/ppermute | solution.py:13
  15.8 407.1 %collective-permute-start = (bf16[24,3072]{1,0:T(8,128)(2,1)}, bf16[24,3072]{1,0:T(8,128)(2,1)}, u32[]{:S(2)}, u32[]{:S(2)}) collective-permute-start(bf16[24,3072]{1,0:T(8,128)(2,1)} %slice_bitcast_fusion.8), channel_id=1, source_target_pairs={{0,4},{1,5},{2,6},{3,7},{4,0},{5,1},{6,2},{7,3},{8,12},{9,13},{10,... | collective-permute-start | bytes 442376 | tf_op jit(solution)/shard_map/ppermute | solution.py:13
  29.0 3.8 copy-start.3
  29.0 4.1 copy-start.4
  425.9 4.7 copy-start
  460.4 566.6 %collective-permute-start.3 = (bf16[24,3072]{1,0:T(8,128)(2,1)S(1)}, bf16[24,3072]{1,0:T(8,128)(2,1)S(1)}, u32[]{:S(2)}, u32[]{:S(2)}) collective-permute-start(bf16[24,3072]{1,0:T(8,128)(2,1)S(1)} %bitcast.123), channel_id=1, source_target_pairs={{0,4},{1,5},{2,6},{3,7},{4,0},{5,1},{6,2},{7,3},{8,12},{9,13},{10,... | collective-permute-start | bytes 442376 | tf_op jit(solution)/shard_map/ppermute | solution.py:13
  467.8 560.2 %collective-permute-start.4 = (bf16[24,3072]{1,0:T(8,128)(2,1)S(1)}, bf16[24,3072]{1,0:T(8,128)(2,1)S(1)}, u32[]{:S(2)}, u32[]{:S(2)}) collective-permute-start(bf16[24,3072]{1,0:T(8,128)(2,1)S(1)} %bitcast.124), channel_id=1, source_target_pairs={{0,4},{1,5},{2,6},{3,7},{4,0},{5,1},{6,2},{7,3},{8,12},{9,13},{10,... | collective-permute-start | bytes 442376 | tf_op jit(solution)/shard_map/ppermute | solution.py:13
where the time goes:
time: 1030 us
  blocking collectives  938 us (91%)
  matrix products  29.7 us (3%)
  starting transfers between devices  26.8 us (3%)
  local copies, waits for them, and re-layouts  15.7 us (2%)
  other arithmetic  15.7 us (2%)
    unnamed x2, blocking collectives  757 us
    psum x1, blocking collectives, body(): summed = lax.psum((term_query, term_key), 'group')  181 us
    ppermute x5, starting transfers between devices, swapped(): lax.ppermute(value, axis, [(i, i ^ 1 << distance) for i in range(lax.axis...  26.8 us
  transfers between devices with their start and end apart: 5, of which 0 were waited for; matrix products, arithmetic and copies ran while one was open for 3% of the time, Pallas kernels for 0%

commit v1 on v0

v1 whole, which is shorter than its diff:
```python
import functools
import math

import jax
import jax.numpy as jnp
from jax import lax
from jax.experimental import pallas as pl
from jax.experimental.pallas import tpu as pltpu
from jax.sharding import PartitionSpec as P

DH = 128
EPSILON = 1e-06
SCALE = DH ** (-0.5)
EXP_SCALE = SCALE * math.log2(math.e)
MESH = pl.DeviceIdType.MESH


def normalize(values):
    center = values - jnp.sum(values, axis=-1, keepdims=True) * (1.0 / DH)
    variance = jnp.sum(center * center, axis=-1, keepdims=True) * (1.0 / DH)
    inverse = lax.rsqrt(variance + EPSILON)
    return center * inverse, inverse


def norm_backward(grad_normed, row_hat, inverse, gain):
    cross = grad_normed * row_hat
    grad_hat = grad_normed * gain
    mean_grad = jnp.sum(grad_hat, axis=-1, keepdims=True) * (1.0 / DH)
    mean_cross = jnp.sum(cross * gain, axis=-1, keepdims=True) * (1.0 / DH)
    grad = (grad_hat - mean_grad - row_hat * mean_cross) * inverse
    return grad.astype(jnp.bfloat16), jnp.sum(cross, axis=0, keepdims=True)


def dot(left, right, left_dim, right_dim):
    return lax.dot_general(
        left, right, (((left_dim,), (right_dim,)), ((), ())), preferred_element_type=jnp.float32
    )


def kernel(
    sizes,
    q_hbm,
    k_hbm,
    v_hbm,
    g_hbm,
    gain_q_ref,
    gain_k_ref,
    sizes_ref,
    sends_ref,
    dq_hbm,
    dk_hbm,
    gains_out,
    q_buf,
    k_buf,
    v_buf,
    g_buf,
    q_hat,
    k_hat,
    q_inv,
    k_inv,
    dq_buf,
    dk_buf,
    same,
    tail_out,
    tail_in,
    parts,
    gains,
    terms,
    first,
    last,
    load_sem,
    store_sem,
    parts_sem,
    gains_sem,
    tail_send,
    tail_recv,
    first_sem,
    last_sem,
):
    heads, quarters, groups, rows, tail = sizes
    pairs = heads // 2
    crew = quarters * groups
    keep = rows - tail
    f = lax.axis_index("fsdp")
    g = lax.axis_index("group")
    head = f // quarters
    quarter = f % quarters
    mine = quarter * groups + g
    partner = (f, (g + groups // 2) % groups)

    def head_peer(step):
        other = (head + step) % heads
        return other, (other * quarters + quarter, g)

    def crew_peer(step):
        other = (mine + step) % crew
        return other, (head * quarters + other // groups, other % groups)

    def quarter_peer(step):
        other = (quarter + step) % quarters
        return other, (head * quarters + other, g)

    barrier = pltpu.get_barrier_semaphore()

    def greet_head(step, carry):
        pl.semaphore_signal(barrier, inc=1, device_id=head_peer(step)[1], device_id_type=MESH)
        return carry

    def greet_crew(step, carry):
        pl.semaphore_signal(barrier, inc=1, device_id=crew_peer(step)[1], device_id_type=MESH)
        return carry

    lax.fori_loop(1, heads, greet_head, 0)
    lax.fori_loop(1, crew, greet_crew, 0)

    loads = [
        pltpu.make_async_copy(src, dst, load_sem.at[i])
        for i, (src, dst) in enumerate(
            ((g_hbm, g_buf), (q_hbm, q_buf), (k_hbm, k_buf), (v_hbm, v_buf))
        )
    ]
    for load in loads:
        load.start()

    lane_quarter = lax.broadcasted_iota(jnp.int32, (1, DH), 1) // (DH // quarters)
    own_gains = jnp.concatenate(
        [
            jnp.concatenate([gain_ref[...]] * quarters, axis=1)
            for gain_ref in (gain_q_ref, gain_k_ref)
        ],
        axis=0,
    )
    parts[quarter] = jnp.where(lane_quarter == quarter, own_gains, 0.0)

    row_ids = jnp.zeros((rows, rows), jnp.int32)
    col_ids = jnp.zeros((rows, rows), jnp.int32)
    row_place = lax.broadcasted_iota(jnp.int32, (rows, rows), 0)
    col_place = lax.broadcasted_iota(jnp.int32, (rows, rows), 1)
    end = jnp.int32(0)
    for i in range(sizes_ref.shape[1]):
        end = end + sizes_ref[0, i]
        row_ids += (row_place >= end).astype(jnp.int32)
        col_ids += (col_place >= end).astype(jnp.int32)
    same[...] = (row_ids == col_ids).astype(jnp.float32)

    loads[0].wait()

    def pack_tail(pair, carry):
        lanes = pl.ds(pl.multiple_of(pair * 2 * DH, 2 * DH), 2 * DH)
        block = g_buf[rows : rows + tail, lanes].astype(jnp.float32)
        stacked = jnp.concatenate([block[:, :DH], block[:, DH:]], axis=0)
        tail_out[pair] = stacked.astype(jnp.bfloat16)
        return carry

    lax.fori_loop(0, pairs, pack_tail, 0)

    pl.semaphore_wait(barrier, heads - 1 + crew - 1)

    def send_part(step, carry):
        pltpu.make_async_remote_copy(
            src_ref=parts.at[quarter],
            dst_ref=parts.at[quarter],
            send_sem=parts_sem.at[0],
            recv_sem=parts_sem.at[1],
            device_id=quarter_peer(step)[1],
            device_id_type=MESH,
        ).start()
        return carry

    lax.fori_loop(1, quarters, send_part, 0)

    def pair_at(step):
        return (head // 2 + 1 + step) % pairs

    def tail_copy(step):
        pair = pair_at(step)
        return pltpu.make_async_remote_copy(
            src_ref=tail_out.at[pair],
            dst_ref=tail_in.at[pair],
            send_sem=tail_send.at[step],
            recv_sem=tail_recv.at[step],
            device_id=partner,
            device_id_type=MESH,
        )

    def send_tail(step, carry):
        tail_copy(step).start()
        return carry

    def wait_all(buffer, count, sem):
        span = buffer.at[pl.ds(0, count)]
        pltpu.make_async_copy(span, span, sem).wait()

    wait_all(parts, quarters - 1, parts_sem.at[0])
    wait_all(parts, quarters - 1, parts_sem.at[1])
    gains[head] = jnp.sum(parts[...], axis=0)

    def send_gain(step, carry):
        pltpu.make_async_remote_copy(
            src_ref=gains.at[head],
            dst_ref=gains.at[head],
            send_sem=gains_sem.at[0],
            recv_sem=gains_sem.at[1],
            device_id=head_peer(step)[1],
            device_id_type=MESH,
        ).start()
        return carry

    lax.fori_loop(1, heads, send_gain, 0)
    lax.fori_loop(0, pairs, send_tail, 0)

    loads[1].wait()
    loads[2].wait()

    def normalize_pair(pair, carry):
        for half in range(2):
            lanes = pl.ds(pl.multiple_of((pair * 2 + half) * DH, DH), DH)
            for src, hat, inv in ((q_buf, q_hat, q_inv), (k_buf, k_hat, k_inv)):
                row_hat, inverse = normalize(src[:, lanes].astype(jnp.float32))
                hat[:, lanes] = row_hat
                inv[:, lanes] = jnp.broadcast_to(inverse, row_hat.shape)
        return carry

    lax.fori_loop(0, pairs, normalize_pair, 0)
    loads[3].wait()
    wait_all(gains, heads - 1, gains_sem.at[0])
    wait_all(gains, heads - 1, gains_sem.at[1])

    sender = jnp.broadcast_to(sends_ref[0, 0], (tail, DH)) == 1
    low = keep // 16 * 16
    fixed = keep - low

    def attend(index, moved):
        lanes = pl.ds(pl.multiple_of(index * DH, DH), DH)
        gain_q = gains[index, 0:1, :]
        gain_k = gains[index, 1:2, :]
        edge = g_buf[low:rows, lanes].astype(jnp.float32)
        edge = jnp.concatenate([edge[:fixed], jnp.where(sender, moved, edge[fixed:])], axis=0)
        grads = jnp.concatenate([g_buf[:low, lanes], edge.astype(jnp.bfloat16)], axis=0)
        query_hat = q_hat[:, lanes]
        key_hat = k_hat[:, lanes]
        query_norm = (query_hat * gain_q).astype(jnp.bfloat16)
        key_norm = (key_hat * gain_k).astype(jnp.bfloat16)
        scores = dot(query_norm, key_norm, 1, 1)
        weights = jnp.exp2(scores * EXP_SCALE) * same[...]
        grad_probs = dot(grads, v_buf[:, lanes], 1, 1)
        scale = 1.0 / jnp.sum(weights, axis=-1, keepdims=True)
        carried = jnp.sum(weights * grad_probs, axis=-1, keepdims=True) * scale
        grad_scores = (weights * (scale * SCALE) * (grad_probs - carried)).astype(jnp.bfloat16)
        grad_qn = dot(grad_scores, key_norm, 1, 0)
        grad_kn = dot(grad_scores, query_norm, 0, 0)
        grad_q, term_q = norm_backward(grad_qn, query_hat, q_inv[:, lanes], gain_q)
        grad_k, term_k = norm_backward(grad_kn, key_hat, k_inv[:, lanes], gain_k)
        dq_buf[:, lanes] = grad_q
        dk_buf[:, lanes] = grad_k
        terms[index, 0:1, :] = term_q
        terms[index, 1:2, :] = term_k

    def attend_pair(step, carry):
        pair = pair_at(step)
        tail_copy(step).wait()
        moved = tail_in[pair].astype(jnp.float32)
        for half in range(2):
            attend(pair * 2 + half, moved[half * tail : (half + 1) * tail])
        lanes = pl.ds(pl.multiple_of(pair * 2 * DH, 2 * DH), 2 * DH)
        pltpu.make_async_copy(dq_buf.at[:, lanes], dq_hbm.at[:, lanes], store_sem.at[0]).start()
        pltpu.make_async_copy(dk_buf.at[:, lanes], dk_hbm.at[:, lanes], store_sem.at[1]).start()
        for half in range(2):
            index = pair * 2 + half

            @pl.when(index != head)
            def _():
                pltpu.make_async_remote_copy(
                    src_ref=terms.at[index],
                    dst_ref=first.at[head],
                    send_sem=first_sem.at[0],
                    recv_sem=first_sem.at[1],
                    device_id=(index * quarters + quarter, g),
                    device_id_type=MESH,
                ).start()

        return carry

    lax.fori_loop(0, pairs, attend_pair, 0)

    first[head] = terms[head]
    wait_all(first, heads - 1, first_sem.at[1])
    last[mine] = jnp.sum(first[...], axis=0)

    def send_last(step, carry):
        pltpu.make_async_remote_copy(
            src_ref=last.at[mine],
            dst_ref=last.at[mine],
            send_sem=last_sem.at[0],
            recv_sem=last_sem.at[1],
            device_id=crew_peer(step)[1],
            device_id_type=MESH,
        ).start()
        return carry

    lax.fori_loop(1, crew, send_last, 0)
    wait_all(first, heads - 1, first_sem.at[0])
    pltpu.make_async_copy(dq_buf, dq_hbm, store_sem.at[0]).wait()
    pltpu.make_async_copy(dk_buf, dk_hbm, store_sem.at[1]).wait()
    wait_all(last, crew - 1, last_sem.at[0])
    wait_all(last, crew - 1, last_sem.at[1])
    total = jnp.sum(last[...], axis=0)
    width = DH // quarters
    piece = jnp.zeros((2, width), jnp.float32)
    for i in range(quarters):
        piece += jnp.where(quarter == i, total[:, i * width : (i + 1) * width], 0.0)
    gains_out[...] = piece


def body(query_rows, key_rows, value_rows, out_grad, query_gain, key_gain, image_sizes, sends_tail):
    _, _, rows, wid = query_rows.shape
    grad_rows = out_grad.shape[2]
    tail = grad_rows - rows
    heads = wid // DH
    quarters = lax.axis_size("fsdp") // heads
    groups = lax.axis_size("group")
    pairs = heads // 2
    crew = quarters * groups
    width = DH // quarters
    any_spec = pl.BlockSpec(memory_space=pltpu.HBM)
    vmem = pl.BlockSpec(memory_space=pltpu.VMEM)
    smem = pl.BlockSpec(memory_space=pltpu.SMEM)
    wide = (rows, wid)
    dma = pltpu.SemaphoreType.DMA
    dq, dk, gains = pl.pallas_call(
        functools.partial(kernel, (heads, quarters, groups, rows, tail)),
        out_shape=(
            jax.ShapeDtypeStruct(wide, jnp.bfloat16),
            jax.ShapeDtypeStruct(wide, jnp.bfloat16),
            jax.ShapeDtypeStruct((2, width), jnp.float32),
        ),
        in_specs=[any_spec] * 4 + [vmem] * 2 + [smem] * 2,
        out_specs=(any_spec, any_spec, vmem),
        scratch_shapes=[
            pltpu.VMEM(wide, jnp.bfloat16),
            pltpu.VMEM(wide, jnp.bfloat16),
            pltpu.VMEM(wide, jnp.bfloat16),
            pltpu.VMEM((grad_rows, wid), jnp.bfloat16),
            pltpu.VMEM(wide, jnp.float32),
            pltpu.VMEM(wide, jnp.float32),
            pltpu.VMEM(wide, jnp.float32),
            pltpu.VMEM(wide, jnp.float32),
            pltpu.VMEM(wide, jnp.bfloat16),
            pltpu.VMEM(wide, jnp.bfloat16),
            pltpu.VMEM((rows, rows), jnp.float32),
            pltpu.VMEM((pairs, 2 * tail, DH), jnp.bfloat16),
            pltpu.VMEM((pairs, 2 * tail, DH), jnp.bfloat16),
            pltpu.VMEM((quarters, 2, DH), jnp.float32),
            pltpu.VMEM((heads, 2, DH), jnp.float32),
            pltpu.VMEM((heads, 2, DH), jnp.float32),
            pltpu.VMEM((heads, 2, DH), jnp.float32),
            pltpu.VMEM((crew, 2, DH), jnp.float32),
            dma((4,)),
            dma((2,)),
            dma((2,)),
            dma((2,)),
            dma((pairs,)),
            dma((pairs,)),
            dma((2,)),
            dma((2,)),
        ],
        compiler_params=pltpu.CompilerParams(
            collective_id=0, has_side_effects=True, vmem_limit_bytes=48 * 1024 * 1024
        ),
    )(
        query_rows.reshape(wide),
        key_rows.reshape(wide),
        value_rows.reshape(wide),
        out_grad.reshape(grad_rows, wid),
        query_gain.reshape(1, width),
        key_gain.reshape(1, width),
        image_sizes.reshape(1, -1),
        sends_tail,
    )
    return dq[None, None], dk[None, None], gains[0], gains[1]


def solution(mesh):
    placed = (
        P("fsdp", "group", None, None),
        P("fsdp", "group", None, None),
        P("fsdp", "group", None, None),
        P("fsdp", "group", None, None),
        P("fsdp"),
        P("fsdp"),
        P("fsdp", "group", None),
        P("fsdp", "group"),
    )
    return jax.shard_map(
        body,
        mesh=mesh,
        in_specs=placed,
        out_specs=(
            P("fsdp", "group", None, None),
            P("fsdp", "group", None, None),
            P("fsdp"),
            P("fsdp"),
        ),
        check_vma=False,
    )
```

time: 1030 us -> 60.1 us (0.06)
  blocking collectives: 938 us -> 0 us
  Pallas kernels: 0 us -> 50.9 us
  matrix products: 29.7 us -> 0 us
  starting transfers between devices: 26.8 us -> 0 us
  other arithmetic: 15.7 us -> 0 us
    unnamed x2 -> x0, blocking collectives: 757 us -> none
    psum x1 -> x0, blocking collectives: 181 us -> none  [body(): summed = lax.psum((term_query, term_key), 'group')]
    pallas_call x0 -> x1, Pallas kernels: none -> 50.9 us  [body(): pl.pallas_call(functools.partial(kernel, (heads, quarters, groups, rows,...]
    dot_general x4 -> x0, matrix products: 29.7 us -> none  [the longest x1 12 us: attend(): jnp.einsum('hqk,khd->qhd', grad_scores, key_norm, preferred_element_type=...]
    ppermute x5 -> x0, starting transfers between devices: 26.8 us -> none  [swapped(): lax.ppermute(value, axis, [(i, i ^ 1 << distance) for i in range(lax.axis...]
  transfers between devices with their start and end apart: 5 -> 0, of which waited for: 0 -> 0; matrix products, arithmetic and copies ran while one was open for 3% -> 0% of each run, Pallas kernels for 0% -> 0%
where the time goes in v1:
time: 60.1 us; the launch traced here: 59.7 us
  Pallas kernels  50.9 us (85%)
  local copies, waits for them, and re-layouts  7.52 us (13%)
  between operations  1.32 us (2%)
    pallas_call x1, Pallas kernels, body(): pl.pallas_call(functools.partial(kernel, (heads, quarters, groups, rows,...  50.9 us
    unnamed x16, local copies, waits for them, and re-layouts  7 us

profile of v1, /device:TPU:1, one launch (start us, length us, event | category | flops | bytes accessed | tf_op | source)
XLA Modules:
  0.0 59.7 jit_solution(1730386750701730321)
XLA Ops:
  1.3 0.0 copy-start.4
  1.3 0.0 copy-start.5
  1.3 0.0 copy-start.6
  1.3 0.6 %copy-done.4 = f32[32]{0:T(128)S(1)} copy-done((f32[32]{0:T(128)S(1)}, f32[32]{0:T(128)}, u32[]{:S(2)}) %copy-start.4) | copy-done | bytes 152
  1.9 0.0 copy-done.5
  2.0 0.0 copy-done.6
  2.0 0.0 copy-start
  2.0 1.2 %copy-done = bf16[1,1,152,3072]{3,2,1,0:T(8,128)(2,1)S(1)} copy-done((bf16[1,1,152,3072]{3,2,1,0:T(8,128)(2,1)S(1)}, bf16[1,1,152,3072]{3,2,1,0:T(8,128)(2,1)}, u32[]{:S(2)}) %copy-start) | copy-done | bytes 933912
  3.2 0.0 copy-start.1
  3.2 1.1 %copy-done.1 = bf16[1,1,128,3072]{3,2,1,0:T(8,128)(2,1)S(1)} copy-done((bf16[1,1,128,3072]{3,2,1,0:T(8,128)(2,1)S(1)}, bf16[1,1,128,3072]{3,2,1,0:T(8,128)(2,1)}, u32[]{:S(2)}) %copy-start.1) | copy-done | bytes 786456
  4.3 0.0 copy-start.2
  4.3 1.1 %copy-done.2 = bf16[1,1,128,3072]{3,2,1,0:T(8,128)(2,1)S(1)} copy-done((bf16[1,1,128,3072]{3,2,1,0:T(8,128)(2,1)S(1)}, bf16[1,1,128,3072]{3,2,1,0:T(8,128)(2,1)}, u32[]{:S(2)}) %copy-start.2) | copy-done | bytes 786456
  5.4 0.0 copy-start.3
  5.4 1.1 %copy-done.3 = bf16[1,1,128,3072]{3,2,1,0:T(8,128)(2,1)S(1)} copy-done((bf16[1,1,128,3072]{3,2,1,0:T(8,128)(2,1)S(1)}, bf16[1,1,128,3072]{3,2,1,0:T(8,128)(2,1)}, u32[]{:S(2)}) %copy-start.3) | copy-done | bytes 786456
  6.6 50.9 %shard_map.111 = (bf16[128,3072]{1,0:T(8,128)(2,1)S(1)}, bf16[128,3072]{1,0:T(8,128)(2,1)S(1)}, f32[2,32]{1,0:T(2,128)S(1)}) custom-call(bf16[128,3072]{1,0:T(8,128)(2,1)S(1)} %bitcast.16, bf16[128,3072]{1,0:T(8,128)(2,1)S(1)} %bitcast.17, bf16[128,3072]{1,0:T(8,128)(2,1)S(1)} %bitcast.18, bf16[152,3072]{1,0:T(8,128)(2,1)S(1)} %bitcast.13, ...), custom_call_target="tpu_custom_call" | custom-call | tf_op jit(solution)/shard_map/pallas_call | solution.py:330
  57.5 0.5 slice_bitcast_fusion
  58.0 0.9 %copy.15 = bf16[1,1,128,3072]{3,2,1,0:T(8,128)(2,1)} copy(bf16[1,1,128,3072]{3,2,1,0:T(8,128)(2,1)S(1)} %bitcast.15) | data formatting | bytes 1572864
  58.9 0.9 %copy.16 = bf16[1,1,128,3072]{3,2,1,0:T(8,128)(2,1)} copy(bf16[1,1,128,3072]{3,2,1,0:T(8,128)(2,1)S(1)} %bitcast.14) | data formatting | bytes 1572864
Async XLA Ops:
  1.3 0.7 %copy-start.4 = (f32[32]{0:T(128)S(1)}, f32[32]{0:T(128)}, u32[]{:S(2)}) copy-start(f32[32]{0:T(128)} %param.12) | copy-start | bytes 388
  1.3 0.7 %copy-start.5 = (f32[32]{0:T(128)S(1)}, f32[32]{0:T(128)}, u32[]{:S(2)}) copy-start(f32[32]{0:T(128)} %param.13) | copy-start | bytes 388
  1.3 0.7 %copy-start.6 = (s32[1,1,4]{2,1,0:T(1,128)S(1)}, s32[1,1,4]{2,1,0:T(1,128)}, u32[]{:S(2)}) copy-start(s32[1,1,4]{2,1,0:T(1,128)} %param.14) | copy-start | bytes 52
  2.0 1.2 %copy-start = (bf16[1,1,152,3072]{3,2,1,0:T(8,128)(2,1)S(1)}, bf16[1,1,152,3072]{3,2,1,0:T(8,128)(2,1)}, u32[]{:S(2)}) copy-start(bf16[1,1,152,3072]{3,2,1,0:T(8,128)(2,1)} %param.11) | copy-start | bytes 2801668
  3.2 1.1 %copy-start.1 = (bf16[1,1,128,3072]{3,2,1,0:T(8,128)(2,1)S(1)}, bf16[1,1,128,3072]{3,2,1,0:T(8,128)(2,1)}, u32[]{:S(2)}) copy-start(bf16[1,1,128,3072]{3,2,1,0:T(8,128)(2,1)} %param.8) | copy-start | bytes 2359300
  4.3 1.1 %copy-start.2 = (bf16[1,1,128,3072]{3,2,1,0:T(8,128)(2,1)S(1)}, bf16[1,1,128,3072]{3,2,1,0:T(8,128)(2,1)}, u32[]{:S(2)}) copy-start(bf16[1,1,128,3072]{3,2,1,0:T(8,128)(2,1)} %param.9) | copy-start | bytes 2359300
  5.4 1.1 %copy-start.3 = (bf16[1,1,128,3072]{3,2,1,0:T(8,128)(2,1)S(1)}, bf16[1,1,128,3072]{3,2,1,0:T(8,128)(2,1)}, u32[]{:S(2)}) copy-start(bf16[1,1,128,3072]{3,2,1,0:T(8,128)(2,1)} %param.10) | copy-start | bytes 2359300

commit v2 on v1

v2 whole, which is shorter than its diff:
```python
import functools
import math

import jax
import jax.numpy as jnp
from jax import lax
from jax.experimental import pallas as pl
from jax.experimental.pallas import tpu as pltpu
from jax.sharding import PartitionSpec as P

DH = 128
EPSILON = 1e-06
SCALE = DH ** (-0.5)
EXP_SCALE = SCALE * math.log2(math.e)
MESH = pl.DeviceIdType.MESH
CHUNKS = 4
VMEM_LIMIT = 48 * 1024 * 1024


def normalize(values):
    center = values - jnp.sum(values, axis=-1, keepdims=True) * (1.0 / DH)
    variance = jnp.sum(center * center, axis=-1, keepdims=True) * (1.0 / DH)
    inverse = lax.rsqrt(variance + EPSILON)
    return center * inverse, inverse


def norm_backward(grad_normed, row_hat, inverse, gain):
    cross = grad_normed * row_hat
    grad_hat = grad_normed * gain
    mean_grad = jnp.sum(grad_hat, axis=-1, keepdims=True) * (1.0 / DH)
    mean_cross = jnp.sum(cross * gain, axis=-1, keepdims=True) * (1.0 / DH)
    grad = (grad_hat - mean_grad - row_hat * mean_cross) * inverse
    return grad.astype(jnp.bfloat16), jnp.sum(cross, axis=0, keepdims=True)


def dot(left, right, right_dim):
    return lax.dot_general(
        left, right, (((1,), (right_dim,)), ((), ())), preferred_element_type=jnp.float32
    )


def diagonal(first, second):
    zero = jnp.zeros_like(first)
    return jnp.concatenate(
        [jnp.concatenate([first, zero], axis=1), jnp.concatenate([zero, second], axis=1)], axis=0
    )


def side_by_side(pieces):
    return jnp.concatenate(pieces, axis=1)


def kernel(
    sizes,
    q_hbm,
    k_hbm,
    v_hbm,
    g_hbm,
    gain_q_hbm,
    gain_k_hbm,
    sizes_hbm,
    sends_ref,
    dq_out,
    dk_out,
    gains_out,
    q_buf,
    k_buf,
    v_buf,
    g_buf,
    gain_buf,
    sizes_buf,
    q_hat,
    k_hat,
    q_inv,
    k_inv,
    dq_buf,
    dk_buf,
    same,
    tail_out,
    tail_in,
    parts,
    gains,
    terms,
    first,
    last,
    load_sem,
    store_sem,
    parts_sem,
    gains_send,
    gains_recv,
    tail_send,
    tail_recv,
    first_sem,
    last_sem,
):
    heads, quarters, groups, rows, tail = sizes
    pairs = heads // 2
    width = DH // quarters
    crew = quarters * groups
    keep = rows - tail
    f = lax.axis_index("fsdp")
    g = lax.axis_index("group")
    head = f // quarters
    quarter = f % quarters
    mine = quarter * groups + g
    partner = (f, (g + groups // 2) % groups)

    def by_line(action, lines):
        def visit(step, carry):
            for other in (lines(step), lines(step) + pairs):
                pl.when(other != head)(functools.partial(action, (other * quarters + quarter, g)))
            return carry

        lax.fori_loop(0, pairs, visit, 0)

    def crew_peer(step):
        other = (mine + step) % crew
        return (head * quarters + other // groups, other % groups)

    def quarter_peer(step):
        return (head * quarters + (quarter + step) % quarters, g)

    barrier = pltpu.get_barrier_semaphore()

    def greet(peer):
        def signal(step, carry):
            pl.semaphore_signal(barrier, inc=1, device_id=peer(step), device_id_type=MESH)
            return carry

        return signal

    by_line(
        lambda peer: pl.semaphore_signal(barrier, inc=1, device_id=peer, device_id_type=MESH),
        lambda step: step,
    )
    lax.fori_loop(1, crew, greet(crew_peer), 0)

    loads = [
        pltpu.make_async_copy(src, dst, load_sem.at[i])
        for i, (src, dst) in enumerate(
            (
                (gain_q_hbm, gain_buf.at[0]),
                (gain_k_hbm, gain_buf.at[1]),
                (sizes_hbm, sizes_buf),
                (g_hbm, g_buf),
                (q_hbm, q_buf),
                (k_hbm, k_buf),
                (v_hbm, v_buf),
            )
        )
    ]
    for load in loads:
        load.start()
    for load in loads[:3]:
        load.wait()

    lane_quarter = lax.broadcasted_iota(jnp.int32, (1, DH), 1) // width
    own_gains = jnp.concatenate([side_by_side([gain_buf[i]] * quarters) for i in range(2)], axis=0)
    parts[quarter] = jnp.where(lane_quarter == quarter, own_gains, 0.0)

    row_ids = jnp.zeros((rows, rows), jnp.int32)
    col_ids = jnp.zeros((rows, rows), jnp.int32)
    row_place = lax.broadcasted_iota(jnp.int32, (rows, rows), 0)
    col_place = lax.broadcasted_iota(jnp.int32, (rows, rows), 1)
    end = jnp.int32(0)
    for i in range(sizes_buf.shape[1]):
        end = end + sizes_buf[0, i]
        row_ids += (row_place >= end).astype(jnp.int32)
        col_ids += (col_place >= end).astype(jnp.int32)
    same[...] = (row_ids == col_ids).astype(jnp.float32)

    def lanes_of(index):
        return pl.ds(pl.multiple_of(index * DH, DH), DH)

    loads[3].wait()

    def pack_tail(pair, carry):
        stacked = jnp.concatenate(
            [g_buf[rows : rows + tail, lanes_of(pair + i * pairs)] for i in range(2)], axis=1
        ).astype(jnp.float32)
        stacked = jnp.concatenate([stacked[:, :DH], stacked[:, DH:]], axis=0)
        tail_out[pair] = stacked.astype(jnp.bfloat16)
        return carry

    lax.fori_loop(0, pairs, pack_tail, 0)

    def normalize_all(src, hat, inv):
        def normalize_pair(pair, carry):
            for i in range(2):
                lanes = lanes_of(pair * 2 + i)
                row_hat, inverse = normalize(src[:, lanes].astype(jnp.float32))
                hat[:, lanes] = row_hat
                inv[:, lanes] = jnp.broadcast_to(inverse, row_hat.shape)
            return carry

        lax.fori_loop(0, pairs, normalize_pair, 0)

    loads[4].wait()
    normalize_all(q_buf, q_hat, q_inv)

    pl.semaphore_wait(barrier, heads - 1 + crew - 1)

    def send_part(step, carry):
        pltpu.make_async_remote_copy(
            src_ref=parts.at[quarter],
            dst_ref=parts.at[quarter],
            send_sem=parts_sem.at[0],
            recv_sem=parts_sem.at[1],
            device_id=quarter_peer(step),
            device_id_type=MESH,
        ).start()
        return carry

    lax.fori_loop(1, quarters, send_part, 0)

    def pair_at(step):
        return step

    def tail_copy(step):
        pair = pair_at(step)
        return pltpu.make_async_remote_copy(
            src_ref=tail_out.at[pair],
            dst_ref=tail_in.at[pair],
            send_sem=tail_send.at[step],
            recv_sem=tail_recv.at[step],
            device_id=partner,
            device_id_type=MESH,
        )

    def send_tail(step, carry):
        tail_copy(step).start()
        return carry

    lax.fori_loop(0, pairs, send_tail, 0)

    def wait_all(buffer, count, sem):
        span = buffer.at[pl.ds(0, count)]
        pltpu.make_async_copy(span, span, sem).wait()

    loads[5].wait()
    normalize_all(k_buf, k_hat, k_inv)

    wait_all(parts, quarters - 1, parts_sem.at[1])
    gains[head] = jnp.sum(parts[...], axis=0)

    def send_gain(peer):
        pltpu.make_async_remote_copy(
            src_ref=gains.at[head],
            dst_ref=gains.at[head],
            send_sem=gains_send.at[0],
            recv_sem=gains_recv.at[head],
            device_id=peer,
            device_id_type=MESH,
        ).start()

    by_line(send_gain, lambda step: pairs - 1 - step)

    loads[6].wait()
    sender = jnp.broadcast_to(sends_ref[0, 0], (tail, 2 * DH)) == 1
    low = keep // 16 * 16
    fixed = keep - low

    def attend(pair):
        indices = (pair, pair + pairs)
        lanes = [lanes_of(i) for i in indices]
        gain_q = [gains[i, 0:1, :] for i in indices]
        gain_k = [gains[i, 1:2, :] for i in indices]
        moved = tail_in[pair].astype(jnp.float32)
        moved = side_by_side([moved[:tail], moved[tail:]])
        edge = side_by_side([g_buf[low:rows, at] for at in lanes]).astype(jnp.float32)
        edge = jnp.concatenate([edge[:fixed], jnp.where(sender, moved, edge[fixed:])], axis=0)
        grads = side_by_side([g_buf[:low, at] for at in lanes])
        grads = jnp.concatenate([grads, edge.astype(jnp.bfloat16)], axis=0)
        query_hat = [q_hat[:, at] for at in lanes]
        key_hat = [k_hat[:, at] for at in lanes]
        query_norm = [(hat * gain).astype(jnp.bfloat16) for hat, gain in zip(query_hat, gain_q)]
        key_norm = [(hat * gain).astype(jnp.bfloat16) for hat, gain in zip(key_hat, gain_k)]
        keys = diagonal(*key_norm)
        scores = dot(side_by_side(query_norm), keys, 1)
        grad_probs = dot(grads, diagonal(*[v_buf[:, at] for at in lanes]), 1)
        grad_scores = []
        for i in range(2):
            half = slice(i * rows, (i + 1) * rows)
            weights = jnp.exp2(scores[:, half] * EXP_SCALE) * same[...]
            probs = grad_probs[:, half]
            scale = 1.0 / jnp.sum(weights, axis=-1, keepdims=True)
            carried = jnp.sum(weights * probs, axis=-1, keepdims=True) * scale
            grad_scores.append((weights * (scale * SCALE) * (probs - carried)).astype(jnp.bfloat16))
        grad_qn = dot(side_by_side(grad_scores), keys, 0)
        grad_kn = dot(side_by_side([x.T for x in grad_scores]), diagonal(*query_norm), 0)
        for i, index in enumerate(indices):
            half = slice(i * DH, (i + 1) * DH)
            at = lanes[i]
            grad_q, term_q = norm_backward(grad_qn[:, half], query_hat[i], q_inv[:, at], gain_q[i])
            grad_k, term_k = norm_backward(grad_kn[:, half], key_hat[i], k_inv[:, at], gain_k[i])
            dq_buf[:, at] = grad_q
            dk_buf[:, at] = grad_k
            terms[index, 0:1, :] = term_q
            terms[index, 1:2, :] = term_k

    batch = 2 if pairs % 2 == 0 else 1

    def attend_batch(turn, carry):
        todo = [pair_at(turn * batch + i) for i in range(batch)]
        for i, pair in enumerate(todo):
            for index in (pair, pair + pairs):

                @pl.when(index != head)
                def _():
                    row = gains.at[index]
                    pltpu.make_async_copy(row, row, gains_recv.at[index]).wait()

            tail_copy(turn * batch + i).wait()
        for pair in todo:
            attend(pair)
        for pair in todo:
            for index in (pair, pair + pairs):

                @pl.when(index != head)
                def _():
                    pltpu.make_async_remote_copy(
                        src_ref=terms.at[index],
                        dst_ref=first.at[head],
                        send_sem=first_sem.at[0],
                        recv_sem=first_sem.at[1],
                        device_id=(index * quarters + quarter, g),
                        device_id_type=MESH,
                    ).start()

        for pair in todo:
            for index in (pair, pair + pairs):
                at = lanes_of(index)
                pltpu.make_async_copy(dq_buf.at[:, at], dq_out.at[:, at], store_sem.at[0]).start()
                pltpu.make_async_copy(dk_buf.at[:, at], dk_out.at[:, at], store_sem.at[1]).start()
        return carry

    lax.fori_loop(0, pairs // batch, attend_batch, 0)

    first[head] = terms[head]
    wait_all(first, heads - 1, first_sem.at[1])
    last[mine] = jnp.sum(first[...], axis=0)

    def send_last(step, carry):
        pltpu.make_async_remote_copy(
            src_ref=last.at[mine],
            dst_ref=last.at[mine],
            send_sem=last_sem.at[0],
            recv_sem=last_sem.at[1],
            device_id=crew_peer(step),
            device_id_type=MESH,
        ).start()
        return carry

    lax.fori_loop(1, crew, send_last, 0)
    wait_all(parts, quarters - 1, parts_sem.at[0])
    wait_all(gains, heads - 1, gains_send.at[0])
    wait_all(first, heads - 1, first_sem.at[0])
    pltpu.make_async_copy(dq_buf, dq_out, store_sem.at[0]).wait()
    pltpu.make_async_copy(dk_buf, dk_out, store_sem.at[1]).wait()
    wait_all(last, crew - 1, last_sem.at[0])
    wait_all(last, crew - 1, last_sem.at[1])
    total = jnp.sum(last[...], axis=0)
    piece = jnp.zeros((2, width), jnp.float32)
    for i in range(quarters):
        piece += jnp.where(quarter == i, total[:, i * width : (i + 1) * width], 0.0)
    gains_out[...] = piece


def finish(dq_in, dk_in, gains_in, dq_out, dk_out, gain_q_out, gain_k_out, sem):
    rows = dq_in.shape[0]
    chunk = rows // CHUNKS
    copies = [
        pltpu.make_async_copy(
            src.at[pl.ds(i * chunk, chunk)], dst.at[pl.ds(i * chunk, chunk)], sem.at[j * CHUNKS + i]
        )
        for i in range(CHUNKS)
        for j, (src, dst) in enumerate(((dq_in, dq_out), (dk_in, dk_out)))
    ]
    for copy in copies:
        copy.start()
    gain_q_out[...] = gains_in[0:1, :]
    gain_k_out[...] = gains_in[1:2, :]
    for copy in copies:
        copy.wait()


def body(query_rows, key_rows, value_rows, out_grad, query_gain, key_gain, image_sizes, sends_tail):
    _, _, rows, wid = query_rows.shape
    grad_rows = out_grad.shape[2]
    tail = grad_rows - rows
    heads = wid // DH
    quarters = lax.axis_size("fsdp") // heads
    groups = lax.axis_size("group")
    pairs = heads // 2
    crew = quarters * groups
    width = DH // quarters
    any_spec = pl.BlockSpec(memory_space=pl.ANY)
    vmem = pl.BlockSpec(memory_space=pltpu.VMEM)
    wide = (rows, wid)
    dma = pltpu.SemaphoreType.DMA
    images = image_sizes.shape[-1]
    operands = (
        query_rows.reshape(wide),
        key_rows.reshape(wide),
        value_rows.reshape(wide),
        out_grad.reshape(grad_rows, wid),
        query_gain.reshape(1, width),
        key_gain.reshape(1, width),
        image_sizes.reshape(1, images),
    )
    dq, dk, gains = pl.pallas_call(
        functools.partial(kernel, (heads, quarters, groups, rows, tail)),
        out_shape=(
            jax.ShapeDtypeStruct(wide, jnp.bfloat16),
            jax.ShapeDtypeStruct(wide, jnp.bfloat16),
            jax.ShapeDtypeStruct((2, width), jnp.float32),
        ),
        in_specs=[any_spec] * 7 + [pl.BlockSpec(memory_space=pltpu.SMEM)],
        out_specs=(any_spec, any_spec, vmem),
        scratch_shapes=[
            pltpu.VMEM(wide, jnp.bfloat16),
            pltpu.VMEM(wide, jnp.bfloat16),
            pltpu.VMEM(wide, jnp.bfloat16),
            pltpu.VMEM((grad_rows, wid), jnp.bfloat16),
            pltpu.VMEM((2, 1, width), jnp.float32),
            pltpu.SMEM((1, images), jnp.int32),
            pltpu.VMEM(wide, jnp.float32),
            pltpu.VMEM(wide, jnp.float32),
            pltpu.VMEM(wide, jnp.float32),
            pltpu.VMEM(wide, jnp.float32),
            pltpu.VMEM(wide, jnp.bfloat16),
            pltpu.VMEM(wide, jnp.bfloat16),
            pltpu.VMEM((rows, rows), jnp.float32),
            pltpu.VMEM((pairs, 2 * tail, DH), jnp.bfloat16),
            pltpu.VMEM((pairs, 2 * tail, DH), jnp.bfloat16),
            pltpu.VMEM((quarters, 2, DH), jnp.float32),
            pltpu.VMEM((heads, 2, DH), jnp.float32),
            pltpu.VMEM((heads, 2, DH), jnp.float32),
            pltpu.VMEM((heads, 2, DH), jnp.float32),
            pltpu.VMEM((crew, 2, DH), jnp.float32),
            dma((7,)),
            dma((2,)),
            dma((2,)),
            dma((1,)),
            dma((heads,)),
            dma((pairs,)),
            dma((pairs,)),
            dma((2,)),
            dma((2,)),
        ],
        compiler_params=pltpu.CompilerParams(
            collective_id=0, has_side_effects=True, vmem_limit_bytes=VMEM_LIMIT
        ),
    )(*[pltpu.with_memory_space_constraint(x, pltpu.HBM) for x in operands], sends_tail)
    dq, dk, gain_q, gain_k = pl.pallas_call(
        finish,
        out_shape=(
            jax.ShapeDtypeStruct(wide, jnp.bfloat16),
            jax.ShapeDtypeStruct(wide, jnp.bfloat16),
            jax.ShapeDtypeStruct((1, width), jnp.float32),
            jax.ShapeDtypeStruct((1, width), jnp.float32),
        ),
        in_specs=[vmem, vmem, vmem],
        out_specs=(any_spec, any_spec, vmem, vmem),
        scratch_shapes=[dma((2 * CHUNKS,))],
    )(*[pltpu.with_memory_space_constraint(x, pltpu.VMEM) for x in (dq, dk, gains)])
    return dq[None, None], dk[None, None], gain_q.reshape(width), gain_k.reshape(width)


def solution(mesh):
    placed = (
        P("fsdp", "group", None, None),
        P("fsdp", "group", None, None),
        P("fsdp", "group", None, None),
        P("fsdp", "group", None, None),
        P("fsdp"),
        P("fsdp"),
        P("fsdp", "group", None),
        P("fsdp", "group"),
    )
    return jax.shard_map(
        body,
        mesh=mesh,
        in_specs=placed,
        out_specs=(
            P("fsdp", "group", None, None),
            P("fsdp", "group", None, None),
            P("fsdp"),
            P("fsdp"),
        ),
        check_vma=False,
    )
```

time: 60.1 us -> 46 us (0.77)
  local copies, waits for them, and re-layouts: 7.52 us -> 0 us
  Pallas kernels: 50.9 us -> 44.6 us
    pallas_call x1, Pallas kernels: 50.9 us -> 42.9 us  [body(): pl.pallas_call(functools.partial(kernel, (heads, quarters, groups, rows,...]
    unnamed x16 -> x0, local copies, waits for them, and re-layouts: 7 us -> none
    pallas_call x0 -> x1, Pallas kernels: none -> 1.71 us  [body(): pl.pallas_call(finish, out_shape=(jax.ShapeDtypeStruct(wide, jnp.bfloat16...]
where the time goes in v2:
time: 46 us; the launch traced here: 45.9 us
  Pallas kernels  44.6 us (97%)
  between operations  1.29 us (3%)
    pallas_call x1, Pallas kernels, body(): pl.pallas_call(functools.partial(kernel, (heads, quarters, groups, rows,...  42.9 us
    pallas_call x1, Pallas kernels, body(): pl.pallas_call(finish, out_shape=(jax.ShapeDtypeStruct(wide, jnp.bfloat16...  1.71 us

profile of v2, /device:TPU:1, one launch (start us, length us, event | category | flops | bytes accessed | tf_op | source)
XLA Modules:
  0.0 45.9 jit_solution(10018464060319692180)
XLA Ops:
  1.3 42.9 %shard_map.111 = (bf16[128,3072]{1,0:T(8,128)(2,1)S(1)}, bf16[128,3072]{1,0:T(8,128)(2,1)S(1)}, f32[2,32]{1,0:T(2,128)S(1)}) custom-call(bf16[128,3072]{1,0:T(8,128)(2,1)} %bitcast.12, bf16[128,3072]{1,0:T(8,128)(2,1)} %bitcast.13, bf16[128,3072]{1,0:T(8,128)(2,1)} %bitcast.14, bf16[152,3072]{1,0:T(8,128)(2,1)} %bitcast.11, f32[1,32]{1,0:T(1,128)} %bitcast.15, ...), custom_call_target="tpu_custom_call" | custom-call | tf_op jit(solution)/shard_map/pallas_call | solution.py:411
  44.1 1.7 %shard_map.112 = (bf16[128,3072]{1,0:T(8,128)(2,1)}, bf16[128,3072]{1,0:T(8,128)(2,1)}, f32[1,32]{1,0:T(1,128)}, f32[1,32]{1,0:T(1,128)}) custom-call(bf16[128,3072]{1,0:T(8,128)(2,1)S(1)} %get-tuple-element.11.dq_in, bf16[128,3072]{1,0:T(8,128)(2,1)S(1)} %get-tuple-element.12.dk_in, f32[2,32]{1,0:T(2,128)S(1)} %get-tuple-element.13.gains_in), custom_call_target="tpu_custom_call" | custom-call | tf_op jit(solution)/shard_map/pallas_call | solution.py:455

commit v3 on v2

--- a/solution.py
+++ b/solution.py
@@ -113,27 +113,26 @@
 
         lax.fori_loop(0, pairs, visit, 0)
 
-    def crew_peer(step):
-        other = (mine + step) % crew
-        return (head * quarters + other // groups, other % groups)
+    def far_first(count):
+        return sorted(range(count), key=lambda step: -min(step, count - step))
+
+    crew_peers = [
+        (head * quarters + (quarter + across) % quarters, (g + along) % groups)
+        for along in far_first(groups)
+        for across in far_first(quarters)
+    ][:-1]
 
     def quarter_peer(step):
         return (head * quarters + (quarter + step) % quarters, g)
 
     barrier = pltpu.get_barrier_semaphore()
-
-    def greet(peer):
-        def signal(step, carry):
-            pl.semaphore_signal(barrier, inc=1, device_id=peer(step), device_id_type=MESH)
-            return carry
-
-        return signal
 
     by_line(
         lambda peer: pl.semaphore_signal(barrier, inc=1, device_id=peer, device_id_type=MESH),
         lambda step: step,
     )
-    lax.fori_loop(1, crew, greet(crew_peer), 0)
+    for peer in crew_peers:
+        pl.semaphore_signal(barrier, inc=1, device_id=peer, device_id_type=MESH)
 
     loads = [
         pltpu.make_async_copy(src, dst, load_sem.at[i])
@@ -340,18 +339,15 @@
     wait_all(first, heads - 1, first_sem.at[1])
     last[mine] = jnp.sum(first[...], axis=0)
 
-    def send_last(step, carry):
+    for peer in crew_peers:
         pltpu.make_async_remote_copy(
             src_ref=last.at[mine],
             dst_ref=last.at[mine],
             send_sem=last_sem.at[0],
             recv_sem=last_sem.at[1],
-            device_id=crew_peer(step),
+            device_id=peer,
             device_id_type=MESH,
         ).start()
-        return carry
-
-    lax.fori_loop(1, crew, send_last, 0)
     wait_all(parts, quarters - 1, parts_sem.at[0])
     wait_all(gains, heads - 1, gains_send.at[0])
     wait_all(first, heads - 1, first_sem.at[0])
@@ -363,7 +359,8 @@
     piece = jnp.zeros((2, width), jnp.float32)
     for i in range(quarters):
         piece += jnp.where(quarter == i, total[:, i * width : (i + 1) * width], 0.0)
-    gains_out[...] = piece
+    for i in range(2):
+        gains_out[i] = piece[i : i + 1]
 
 
 def finish(dq_in, dk_in, gains_in, dq_out, dk_out, gain_q_out, gain_k_out, sem):
@@ -376,10 +373,12 @@
         for i in range(CHUNKS)
         for j, (src, dst) in enumerate(((dq_in, dq_out), (dk_in, dk_out)))
     ]
+    copies += [
+        pltpu.make_async_copy(gains_in.at[i], out, sem.at[2 * CHUNKS + i])
+        for i, out in enumerate((gain_q_out, gain_k_out))
+    ]
     for copy in copies:
         copy.start()
-    gain_q_out[...] = gains_in[0:1, :]
-    gain_k_out[...] = gains_in[1:2, :]
     for copy in copies:
         copy.wait()
 
@@ -413,7 +412,7 @@
         out_shape=(
             jax.ShapeDtypeStruct(wide, jnp.bfloat16),
             jax.ShapeDtypeStruct(wide, jnp.bfloat16),
-            jax.ShapeDtypeStruct((2, width), jnp.float32),
+            jax.ShapeDtypeStruct((2, 1, width), jnp.float32),
         ),
         in_specs=[any_spec] * 7 + [pl.BlockSpec(memory_space=pltpu.SMEM)],
         out_specs=(any_spec, any_spec, vmem),
@@ -461,8 +460,8 @@
             jax.ShapeDtypeStruct((1, width), jnp.float32),
         ),
         in_specs=[vmem, vmem, vmem],
-        out_specs=(any_spec, any_spec, vmem, vmem),
-        scratch_shapes=[dma((2 * CHUNKS,))],
+        out_specs=(any_spec,) * 4,
+        scratch_shapes=[dma((2 * CHUNKS + 2,))],
     )(*[pltpu.with_memory_space_constraint(x, pltpu.VMEM) for x in (dq, dk, gains)])
     return dq[None, None], dk[None, None], gain_q.reshape(width), gain_k.reshape(width)
 

time: 46 us -> 45.3 us (0.985)
  Pallas kernels: 44.6 us -> 43.9 us
    pallas_call x1, Pallas kernels: 1.71 us -> 1.22 us  [body(): pl.pallas_call(finish, out_shape=(jax.ShapeDtypeStruct(wide, jnp.bfloat16...]
where the time goes in v3:
time: 45.3 us; the launch traced here: 45.2 us
  Pallas kernels  43.9 us (97%)
  between operations  1.29 us (3%)
    pallas_call x1, Pallas kernels, body(): pl.pallas_call(functools.partial(kernel, (heads, quarters, groups, rows,...  42.6 us
    pallas_call x1, Pallas kernels, body(): pl.pallas_call(finish, out_shape=(jax.ShapeDtypeStruct(wide, jnp.bfloat16...  1.22 us

profile of v3, /device:TPU:1, one launch (start us, length us, event | category | flops | bytes accessed | tf_op | source)
XLA Modules:
  0.0 45.2 jit_solution(8076602929227528117)
XLA Ops:
  1.3 42.6 %shard_map.111 = (bf16[128,3072]{1,0:T(8,128)(2,1)S(1)}, bf16[128,3072]{1,0:T(8,128)(2,1)S(1)}, f32[2,1,32]{2,1,0:T(1,128)S(1)}) custom-call(bf16[128,3072]{1,0:T(8,128)(2,1)} %bitcast.12, bf16[128,3072]{1,0:T(8,128)(2,1)} %bitcast.13, bf16[128,3072]{1,0:T(8,128)(2,1)} %bitcast.14, bf16[152,3072]{1,0:T(8,128)(2,1)} %bitcast.11, f32[1,32]{1,0:T(1,128)} %bitcast.15, ...), custom_call_target="tpu_custom_call" | custom-call | tf_op jit(solution)/shard_map/pallas_call | solution.py:410
  43.9 1.2 %shard_map.112 = (bf16[128,3072]{1,0:T(8,128)(2,1)}, bf16[128,3072]{1,0:T(8,128)(2,1)}, f32[1,32]{1,0:T(1,128)}, f32[1,32]{1,0:T(1,128)}) custom-call(bf16[128,3072]{1,0:T(8,128)(2,1)S(1)} %get-tuple-element.11.dq_in, bf16[128,3072]{1,0:T(8,128)(2,1)S(1)} %get-tuple-element.12.dk_in, f32[2,1,32]{2,1,0:T(1,128)S(1)} %get-tuple-element.13.gains_in), custom_call_target="tpu_custom_call" | custom-call | tf_op jit(solution)/shard_map/pallas_call | solution.py:454

commit v4 on v3

--- a/solution.py
+++ b/solution.py
@@ -297,10 +297,8 @@
             terms[index, 0:1, :] = term_q
             terms[index, 1:2, :] = term_k
 
-    batch = 2 if pairs % 2 == 0 else 1
-
-    def attend_batch(turn, carry):
-        todo = [pair_at(turn * batch + i) for i in range(batch)]
+    def attend_batch(start, count):
+        todo = [pair_at(start + i) for i in range(count)]
         for i, pair in enumerate(todo):
             for index in (pair, pair + pairs):
 
@@ -309,7 +307,7 @@
                     row = gains.at[index]
                     pltpu.make_async_copy(row, row, gains_recv.at[index]).wait()
 
-            tail_copy(turn * batch + i).wait()
+            tail_copy(start + i).wait()
         for pair in todo:
             attend(pair)
         for pair in todo:
@@ -331,9 +329,15 @@
                 at = lanes_of(index)
                 pltpu.make_async_copy(dq_buf.at[:, at], dq_out.at[:, at], store_sem.at[0]).start()
                 pltpu.make_async_copy(dk_buf.at[:, at], dk_out.at[:, at], store_sem.at[1]).start()
+
+    def attend_two(turn, carry):
+        attend_batch(1 + turn * 2, 2)
         return carry
 
-    lax.fori_loop(0, pairs // batch, attend_batch, 0)
+    attend_batch(0, 1)
+    lax.fori_loop(0, (pairs - 1) // 2, attend_two, 0)
+    if pairs % 2 == 0:
+        attend_batch(pairs - 1, 1)
 
     first[head] = terms[head]
     wait_all(first, heads - 1, first_sem.at[1])

time: 45.3 us -> 44.8 us (0.989)
  Pallas kernels: 43.9 us -> 43.4 us
    pallas_call x1, Pallas kernels: 42.6 us -> 42.1 us  [body(): pl.pallas_call(functools.partial(kernel, (heads, quarters, groups, rows,...]
where the time goes in v4:
time: 44.8 us; the launch traced here: 44.6 us
  Pallas kernels  43.4 us (97%)
  between operations  1.29 us (3%)
    pallas_call x1, Pallas kernels, body(): pl.pallas_call(functools.partial(kernel, (heads, quarters, groups, rows,...  42.1 us
    pallas_call x1, Pallas kernels, body(): pl.pallas_call(finish, out_shape=(jax.ShapeDtypeStruct(wide, jnp.bfloat16...  1.22 us

profile of v4, /device:TPU:1, one launch (start us, length us, event | category | flops | bytes accessed | tf_op | source)
XLA Modules:
  0.0 44.6 jit_solution(13001073240633266878)
XLA Ops:
  1.3 42.1 %shard_map.111 = (bf16[128,3072]{1,0:T(8,128)(2,1)S(1)}, bf16[128,3072]{1,0:T(8,128)(2,1)S(1)}, f32[2,1,32]{2,1,0:T(1,128)S(1)}) custom-call(bf16[128,3072]{1,0:T(8,128)(2,1)} %bitcast.12, bf16[128,3072]{1,0:T(8,128)(2,1)} %bitcast.13, bf16[128,3072]{1,0:T(8,128)(2,1)} %bitcast.14, bf16[152,3072]{1,0:T(8,128)(2,1)} %bitcast.11, f32[1,32]{1,0:T(1,128)} %bitcast.15, ...), custom_call_target="tpu_custom_call" | custom-call | tf_op jit(solution)/shard_map/pallas_call | solution.py:414
  43.4 1.2 %shard_map.112 = (bf16[128,3072]{1,0:T(8,128)(2,1)}, bf16[128,3072]{1,0:T(8,128)(2,1)}, f32[1,32]{1,0:T(1,128)}, f32[1,32]{1,0:T(1,128)}) custom-call(bf16[128,3072]{1,0:T(8,128)(2,1)S(1)} %get-tuple-element.11.dq_in, bf16[128,3072]{1,0:T(8,128)(2,1)S(1)} %get-tuple-element.12.dk_in, f32[2,1,32]{2,1,0:T(1,128)S(1)} %get-tuple-element.13.gains_in), custom_call_target="tpu_custom_call" | custom-call | tf_op jit(solution)/shard_map/pallas_call | solution.py:458
